TPU v7x, 32 devices: a whole 2x2x4 slice. The times are simulated.
32 devices in a mesh: orb: 8 (over z, y), grid: 4 (over x, core).
Axes of the slice: x: 2, y: 2, z: 4, core: 2. Of those that a mesh axis runs over, the one named last changes fastest.
Arguments:
- orbitals: float32 [16, 32, 1024], P('orb', 'grid'), may hold values from -6 to 6
- dielectric: float32 [16, 32, 1024], P('orb', 'grid'), may hold values from 1 to 80
- pair_offsets: int32 [16, 4], replicated, may hold values from 0 to 3, each once within a row
- pair_counts: int32 [16], replicated, may hold values from 1 to 4, as said below
- box_shift: int32 [16], replicated, may hold values from 0 to 8
Outputs:
- exchange_action: float32 [16, 32, 1024], P('orb', 'grid')
Inputs may be any that keep to these rules, and one draw needn't show every extreme that they name: `pair_counts`: in each aligned block of 8 orbitals the counts sum to 16, and in each such block the 2 orbitals of one owner (an aligned run of 2 orbitals) all have 4. `pair_offsets`: each row is a permutation of 0 to 3; only its first pair_counts entries name pairs.
All inputs are finite; a program needn't handle non-finite values.
Results may differ from a plain program's by a relative error of at most 0.00013.
Values sent between devices are 32-bit elements; how exact they have to be, the bound alone decides.
A program may use at most 64 MiB of HBM per device.

v0:
```python
import jax
import jax.numpy as jnp
from jax import lax
from jax.sharding import PartitionSpec as P

B = 32
PMAX = 4
SMAX = 8
CYCLES = 2
SWEEPS = 4


FOURPI = 4.0 * 3.141592653589793
OMEGA = 0.8
HIGHEST = lax.Precision.HIGHEST


def extended_2(value, sides, width):
    for axis, dim in sides:
        size, length = (lax.axis_size(axis), value.shape[dim])
        up = [(i, (i + 1) % size) for i in range(size - 1)]
        down = [(j, i) for i, j in up]
        last = lax.slice_in_dim(value, length - width, length, axis=dim)
        initial = lax.slice_in_dim(value, 0, width, axis=dim)
        before = lax.ppermute(last, axis, up)
        after = lax.ppermute(initial, axis, down)
        value = jnp.concatenate([before, value, after], axis=dim)
    return value


def passed_along(value, axis, steps):
    count = lax.axis_size(axis)
    pairs = [(source, (source + steps) % count) for source in range(count)]
    return lax.ppermute(value, axis, pairs)


def lookup(table, wanted):
    matches = wanted[:, None] == jnp.arange(table.shape[0], dtype=jnp.int32)[None, :]
    return jnp.sum(jnp.where(matches, table[None, :], 0), axis=1)


def beside_all(extended, edge_cells):
    centre = extended[:, 1:-1]
    column = lax.broadcasted_iota(jnp.int32, centre.shape, 2) % edge_cells
    row_padded = jnp.pad(centre, ((0, 0), (0, 0), (edge_cells, edge_cells)))
    col_padded = jnp.pad(centre, ((0, 0), (0, 0), (1, 1)))
    nothing = jnp.zeros_like(centre)
    neighbours = [
        extended[:, 2:],
        extended[:, :-2],
        row_padded[:, :, 2 * edge_cells :],
        row_padded[:, :, : -2 * edge_cells],
        jnp.where(column < edge_cells - 1, col_padded[:, :, 2:], nothing),
        jnp.where(column > 0, col_padded[:, :, :-2], nothing),
    ]
    return (centre, neighbours)


def diagonal_of(eps_ext, edge_cells, level_scale):
    centre, neighbours = beside_all(eps_ext, edge_cells)
    summed = jnp.zeros_like(centre)
    for eps_next in neighbours:
        summed = summed + 0.5 * (centre + eps_next)
    return level_scale * summed


def operate(values, level_data):
    eps_ext, diagonal, edge_cells, level_scale, whole_box = level_data
    extended = extended_2(values, (("grid", 1),), 1)
    neighbours = beside_all(extended, edge_cells)[1]
    eps_parts = beside_all(eps_ext, edge_cells)
    weighted = jnp.zeros_like(values)
    for eps_next, val_next in zip(eps_parts[1], neighbours):
        weighted = weighted + 0.5 * (eps_parts[0] + eps_next) * val_next
    return diagonal * values - level_scale * weighted


def coarsen(values, edge_cells):
    slot_count, layer_count, plane_cells = values.shape
    half_edge = edge_cells // 2
    grouped = values.reshape(slot_count, layer_count // 2, 2, half_edge, 2, half_edge, 2)
    return grouped.mean(axis=(2, 4, 6)).reshape(slot_count, layer_count // 2, plane_cells // 4)


def refine(values, half_edge):
    slot_count, layer_count, plane_cells = values.shape
    grown = jnp.broadcast_to(
        values.reshape(slot_count, layer_count, 1, half_edge, 1, half_edge, 1),
        (slot_count, layer_count, 2, half_edge, 2, half_edge, 2),
    )
    return grown.reshape(slot_count, 2 * layer_count, 4 * plane_cells)


def relaxed_step(values, rhs_level, level_data):
    diagonal = level_data[1]
    if values is None:
        return OMEGA * rhs_level / diagonal
    return values + OMEGA * (rhs_level - operate(values, level_data)) / diagonal


def multigrid_cycle(depth_index, values, rhs_level, levels):
    level_data = levels[depth_index]
    if depth_index == len(levels) - 1:
        for sweep_index in range(SWEEPS):
            values = relaxed_step(values, rhs_level, level_data)
        return values
    values = relaxed_step(values, rhs_level, level_data)
    residual = rhs_level - operate(values, level_data)
    correction = multigrid_cycle(depth_index + 1, None, coarsen(residual, level_data[2]), levels)
    values = values + refine(correction, level_data[2] // 2)
    return relaxed_step(values, rhs_level, level_data)


def shift_rows(values, row_offset, edge_cells):
    margin_cells = SMAX * edge_cells
    padded = jnp.pad(values, ((0, 0), (0, 0), (margin_cells, margin_cells)))
    plane_cells = values.shape[2]

    def one_slot(single, offset_value):
        return lax.dynamic_slice_in_dim(single, (SMAX + offset_value) * edge_cells, plane_cells, 1)

    return jax.vmap(one_slot)(padded, row_offset)


def solve_pairs(phi_first, second_field, eps_levels, row_offset, live_mask):
    moved = shift_rows(second_field, row_offset, B)
    rhs_fine = FOURPI * (phi_first * moved)
    levels = []
    for level_index in range(3):
        edge_cells = B // 2**level_index
        level_scale = 0.25**level_index
        eps_ext = eps_levels[level_index]
        levels.append(
            (eps_ext, diagonal_of(eps_ext, edge_cells, level_scale), edge_cells, level_scale, False)
        )
    potential = None
    for cycle_index in range(CYCLES):
        potential = multigrid_cycle(0, potential, rhs_fine, levels)
    to_first = -(potential * moved) * live_mask[:, None, None]
    to_second = -shift_rows(potential * phi_first, -row_offset, B) * live_mask[:, None, None]
    return (to_first, to_second)


def shards(orbitals, dielectric, pair_offsets, pair_counts, box_shift):
    owner = lax.axis_index("orb")
    orbital_count = pair_counts.shape[0]
    own_count = orbitals.shape[0]
    deep_rims = extended_2(dielectric, (("grid", 1),), 4)
    eps_fine = deep_rims[:, 3:-3]
    eps_half_deep = coarsen(deep_rims, B)
    eps_quarter = coarsen(eps_half_deep, B // 2)
    eps_half = eps_half_deep[:, 1:-1]
    own_fields = [orbitals, eps_fine, eps_half, eps_quarter]
    field_shapes = [item.shape[1:] for item in own_fields]
    field_sizes = [shape_pair[0] * shape_pair[1] for shape_pair in field_shapes]
    packet = jnp.concatenate([item.reshape(own_count, -1) for item in own_fields], axis=1)
    reach = (PMAX + own_count - 1) // own_count
    lowest = 0
    first_orb = owner * own_count + jnp.repeat(jnp.arange(own_count, dtype=jnp.int32), PMAX)
    pair_rank = jnp.tile(jnp.arange(PMAX, dtype=jnp.int32), own_count)
    live_mask = (pair_rank < lookup(pair_counts, first_orb)).astype(jnp.float32)
    slot_count = first_orb.shape[0]
    distance = 1 + lookup(pair_offsets.reshape(-1), first_orb * PMAX + pair_rank)
    second_orb = (first_orb + distance) % orbital_count
    row_offset = lookup(box_shift, first_orb) - lookup(box_shift, second_orb)
    window_first = (owner + lowest) * own_count
    first_place = (first_orb - window_first) % orbital_count
    second_place = (second_orb - window_first) % orbital_count
    arrived = []
    for offset in range(lowest, reach + 1):
        if offset == 0:
            arrived.append(packet)
        else:
            arrived.append(passed_along(packet, "orb", -offset))
    lane_index = jnp.arange(own_count, dtype=jnp.int32)
    first_fields = [
        jnp.zeros((slot_count,) + tuple(shape_pair), jnp.float32) for shape_pair in field_shapes
    ]
    second_field = jnp.zeros((slot_count,) + tuple(field_shapes[0]), jnp.float32)
    first_hots = []
    second_hots = []
    for block_index in range(reach - lowest + 1):
        targets = block_index * own_count + lane_index
        first_hot = (first_place[:, None] == targets[None, :]).astype(jnp.float32)
        second_hot = (second_place[:, None] == targets[None, :]).astype(jnp.float32)
        first_hots.append(first_hot)
        second_hots.append(second_hot)
        received = arrived[block_index]
        column_start = 0
        for field_index in range(len(field_shapes)):
            portion = received[:, column_start : column_start + field_sizes[field_index]]
            portion = portion.reshape((own_count,) + tuple(field_shapes[field_index]))
            first_fields[field_index] = first_fields[field_index] + jnp.einsum(
                "sa,azf->szf", first_hot, portion, precision=HIGHEST
            )
            if field_index == 0:
                second_field = second_field + jnp.einsum(
                    "sa,azf->szf", second_hot, portion, precision=HIGHEST
                )
            column_start = column_start + field_sizes[field_index]
    phi_first, eps_fine_slots, eps_half_slots, eps_quarter_slots = first_fields
    to_first, to_second = solve_pairs(
        phi_first,
        second_field,
        [eps_fine_slots, eps_half_slots, eps_quarter_slots],
        row_offset,
        live_mask,
    )
    outgoing = []
    for block_index in range(reach - lowest + 1):
        outgoing.append(
            jnp.einsum("sa,szf->azf", first_hots[block_index], to_first, precision=HIGHEST)
            + jnp.einsum("sa,szf->azf", second_hots[block_index], to_second, precision=HIGHEST)
        )
    collected = outgoing[-lowest]
    for offset in range(lowest, reach + 1):
        if offset != 0:
            collected = collected + passed_along(outgoing[offset - lowest], "orb", offset)
    return collected


def solution(mesh):
    placed = (P("orb", "grid", None), P("orb", "grid", None), P(), P(), P())
    return jax.shard_map(
        shards, mesh=mesh, in_specs=placed, out_specs=P("orb", "grid", None), check_vma=False
    )
```

profile of v0, /device:TPU:1, one launch (start us, length us, event | category | flops | bytes accessed | tf_op | source)
XLA Modules:
  0.0 225.2 jit_solution(12804701446936020893)
XLA Ops:
  1.0 4.5 %collective-permute-start = (f32[2,4,1024]{2,0,1:T(2,128)S(1)}, f32[2,4,1024]{2,0,1:T(2,128)S(1)}, u32[]{:S(2)}, u32[]{:S(2)}) collective-permute-start(f32[2,4,1024]{2,0,1:T(2,128)S(1)} %copy.252), channel_id=1, source_target_pairs={{0,1},{1,2},{2,3},{4,5},{5,6},{6,7},{8,9},{9,10},{10,11},{12,13},{... | collective-permute-start | bytes 98312 | tf_op jit(solution)/shard_map/ppermute | solution.py:25
  13.9 9.8 %reshape.292 = f32[2,8,2,16,2,16,2]{6,5,4,3,2,1,0:T(8,128)} reshape(f32[2,16,1024]{2,1,0:T(8,128)S(1)} %copy.133) | data formatting | bytes 262144 | tf_op jit(solution)/shard_map/reshape | solution.py:81
  28.6 4.3 %collective-permute-start.2 = (f32[2,20224]{1,0:T(2,128)S(1)}, f32[2,20224]{1,0:T(2,128)S(1)}, u32[]{:S(2)}, u32[]{:S(2)}) collective-permute-start(f32[2,20224]{1,0:T(2,128)S(1)} %pad_maximum_fusion.10), channel_id=1, source_target_pairs={{0,28},{4,0},{8,4},{12,8},{16,12},{20,16},{24,20},{28,24},{1,29},{... | collective-permute-start | bytes 485384 | tf_op jit(solution)/shard_map/ppermute | solution.py:34
  39.4 17.1 %while.2 = (s32[]{:T(128)}, f32[8,8,1536]{2,0,1:T(8,128)S(1)}, s32[8,3]{0,1:T(4,128)S(1)}, f32[8,8,1024]{2,0,1:T(8,128)S(1)}, s32[]{:T(128)}, /*index=5*/s32[]{:T(128)}) while((s32[]{:T(128)}, f32[8,8,1536]{2,0,1:T(8,128)S(1)}, s32[8,3]{0,1:T(4,128)S(1)}, f32[8,8,1024]{2,0,1:T(8,128)S(1)}, s32[]{:T(128)}, /*index=5*/s32[]{:T(128)}) %tuple.93), condition=%wide.while_cond, body=%wide.while_body.sunk | while | flops 2 | bytes 131197 | solution.py:120
  69.1 5.0 %reduce_sum.95 = f32[8,4,16,16]{0,3,2,1:T(8,128)S(1)} reduce(f32[8,4,2,16,2,16,2]{0,6,5,4,3,2,1:T(2,128)} %bitcast.124, f32[]{:T(128)} %constant.201.clone.1), dimensions={2,4,6}, to_apply=%region_5.6 | reduce | flops 57344 | bytes 294916 | tf_op jit(solution)/shard_map/reduce_sum | solution.py:82
  76.7 4.4 %collective-permute-start.7 = (f32[8,1,256]{2,0,1:T(8,128)S(1)}, f32[8,1,256]{2,0,1:T(8,128)S(1)}, u32[]{:S(2)}, u32[]{:S(2)}) collective-permute-start(f32[8,1,256]{2,0,1:T(8,128)S(1)} %get-tuple-element.139), channel_id=1, source_target_pairs={{0,1},{1,2},{2,3},{4,5},{5,6},{6,7},{8,9},{9,10},{10,11},{12,13},{... | collective-permute-start | bytes 24584 | tf_op jit(solution)/shard_map/ppermute | solution.py:25
  84.4 4.2 %collective-permute-start.9 = (f32[8,1,64]{2,0,1:T(8,128)S(1)}, f32[8,1,64]{2,0,1:T(8,128)S(1)}, u32[]{:S(2)}, u32[]{:S(2)}) collective-permute-start(f32[8,1,64]{2,0,1:T(8,128)S(1)} %get-tuple-element.151), channel_id=1, source_target_pairs={{0,1},{1,2},{2,3},{4,5},{5,6},{6,7},{8,9},{9,10},{10,11},{12,13},{... | collective-permute-start | bytes 6152 | tf_op jit(solution)/shard_map/ppermute | solution.py:25
  91.3 4.2 %collective-permute-start.11 = (f32[8,1,64]{2,0,1:T(8,128)S(1)}, f32[8,1,64]{2,0,1:T(8,128)S(1)}, u32[]{:S(2)}, u32[]{:S(2)}) collective-permute-start(f32[8,1,64]{2,0,1:T(8,128)S(1)} %get-tuple-element.149), channel_id=1, source_target_pairs={{0,1},{1,2},{2,3},{4,5},{5,6},{6,7},{8,9},{9,10},{10,11},{12,13},{... | collective-permute-start | bytes 6152 | tf_op jit(solution)/shard_map/ppermute | solution.py:25
  98.3 4.2 %collective-permute-start.13 = (f32[8,1,64]{2,0,1:T(8,128)S(1)}, f32[8,1,64]{2,0,1:T(8,128)S(1)}, u32[]{:S(2)}, u32[]{:S(2)}) collective-permute-start(f32[8,1,64]{2,0,1:T(8,128)S(1)} %get-tuple-element.147), channel_id=1, source_target_pairs={{0,1},{1,2},{2,3},{4,5},{5,6},{6,7},{8,9},{9,10},{10,11},{12,13},{... | collective-permute-start | bytes 6152 | tf_op jit(solution)/shard_map/ppermute | solution.py:25
  105.7 4.2 %collective-permute-start.15 = (f32[8,1,256]{2,0,1:T(8,128)S(1)}, f32[8,1,256]{2,0,1:T(8,128)S(1)}, u32[]{:S(2)}, u32[]{:S(2)}) collective-permute-start(f32[8,1,256]{2,0,1:T(8,128)S(1)} %get-tuple-element.137), channel_id=1, source_target_pairs={{0,1},{1,2},{2,3},{4,5},{5,6},{6,7},{8,9},{9,10},{10,11},{12,13},{... | collective-permute-start | bytes 24584 | tf_op jit(solution)/shard_map/ppermute | solution.py:25
  111.0 4.1 %broadcast_in_dim.133 = f32[8,4,2,16,2,16,2]{0,6,5,4,3,2,1:T(2,128)} broadcast(f32[8,4,16,16]{0,3,2,1:T(8,128)S(1)} %bitcast.128), dimensions={0,1,3,5} | broadcast | bytes 294912 | tf_op jit(solution)/shard_map/broadcast_in_dim | solution.py:87
  119.9 4.2 %collective-permute-start.17 = (f32[8,1,1024]{2,0,1:T(8,128)S(1)}, f32[8,1,1024]{2,0,1:T(8,128)S(1)}, u32[]{:S(2)}, u32[]{:S(2)}) collective-permute-start(f32[8,1,1024]{2,0,1:T(8,128)S(1)} %get-tuple-element.121), channel_id=1, source_target_pairs={{0,1},{1,2},{2,3},{4,5},{5,6},{6,7},{8,9},{9,10},{10,11},{12,13},{... | collective-permute-start | bytes 98312 | tf_op jit(solution)/shard_map/ppermute | solution.py:25
  127.5 4.2 %collective-permute-start.19 = (f32[8,1,1024]{2,0,1:T(8,128)S(1)}, f32[8,1,1024]{2,0,1:T(8,128)S(1)}, u32[]{:S(2)}, u32[]{:S(2)}) collective-permute-start(f32[8,1,1024]{2,0,1:T(8,128)S(1)} %get-tuple-element.119), channel_id=1, source_target_pairs={{0,1},{1,2},{2,3},{4,5},{5,6},{6,7},{8,9},{9,10},{10,11},{12,13},{... | collective-permute-start | bytes 98312 | tf_op jit(solution)/shard_map/ppermute | solution.py:25
  135.1 4.2 %collective-permute-start.21 = (f32[8,1,1024]{2,0,1:T(8,128)S(1)}, f32[8,1,1024]{2,0,1:T(8,128)S(1)}, u32[]{:S(2)}, u32[]{:S(2)}) collective-permute-start(f32[8,1,1024]{2,0,1:T(8,128)S(1)} %get-tuple-element.117), channel_id=1, source_target_pairs={{0,1},{1,2},{2,3},{4,5},{5,6},{6,7},{8,9},{9,10},{10,11},{12,13},{... | collective-permute-start | bytes 98312 | tf_op jit(solution)/shard_map/ppermute | solution.py:25
  143.3 5.0 %reduce_sum.97 = f32[8,4,16,16]{0,3,2,1:T(8,128)S(1)} reduce(f32[8,4,2,16,2,16,2]{0,6,5,4,3,2,1:T(2,128)} %bitcast.126, f32[]{:T(128)} %constant.201.clone.1), dimensions={2,4,6}, to_apply=%region_7.8 | reduce | flops 57344 | bytes 294916 | tf_op jit(solution)/shard_map/reduce_sum | solution.py:82
  150.8 4.2 %collective-permute-start.23 = (f32[8,1,256]{2,0,1:T(8,128)S(1)}, f32[8,1,256]{2,0,1:T(8,128)S(1)}, u32[]{:S(2)}, u32[]{:S(2)}) collective-permute-start(f32[8,1,256]{2,0,1:T(8,128)S(1)} %get-tuple-element.135), channel_id=1, source_target_pairs={{0,1},{1,2},{2,3},{4,5},{5,6},{6,7},{8,9},{9,10},{10,11},{12,13},{... | collective-permute-start | bytes 24584 | tf_op jit(solution)/shard_map/ppermute | solution.py:25
  158.5 4.2 %collective-permute-start.25 = (f32[8,1,64]{2,0,1:T(8,128)S(1)}, f32[8,1,64]{2,0,1:T(8,128)S(1)}, u32[]{:S(2)}, u32[]{:S(2)}) collective-permute-start(f32[8,1,64]{2,0,1:T(8,128)S(1)} %get-tuple-element.145), channel_id=1, source_target_pairs={{0,1},{1,2},{2,3},{4,5},{5,6},{6,7},{8,9},{9,10},{10,11},{12,13},{... | collective-permute-start | bytes 6152 | tf_op jit(solution)/shard_map/ppermute | solution.py:25
  165.4 4.2 %collective-permute-start.27 = (f32[8,1,64]{2,0,1:T(8,128)S(1)}, f32[8,1,64]{2,0,1:T(8,128)S(1)}, u32[]{:S(2)}, u32[]{:S(2)}) collective-permute-start(f32[8,1,64]{2,0,1:T(8,128)S(1)} %get-tuple-element.143), channel_id=1, source_target_pairs={{0,1},{1,2},{2,3},{4,5},{5,6},{6,7},{8,9},{9,10},{10,11},{12,13},{... | collective-permute-start | bytes 6152 | tf_op jit(solution)/shard_map/ppermute | solution.py:25
  172.4 4.2 %collective-permute-start.29 = (f32[8,1,64]{2,0,1:T(8,128)S(1)}, f32[8,1,64]{2,0,1:T(8,128)S(1)}, u32[]{:S(2)}, u32[]{:S(2)}) collective-permute-start(f32[8,1,64]{2,0,1:T(8,128)S(1)} %get-tuple-element.141), channel_id=1, source_target_pairs={{0,1},{1,2},{2,3},{4,5},{5,6},{6,7},{8,9},{9,10},{10,11},{12,13},{... | collective-permute-start | bytes 6152 | tf_op jit(solution)/shard_map/ppermute | solution.py:25
  179.8 4.2 %collective-permute-start.31 = (f32[8,1,256]{2,0,1:T(8,128)S(1)}, f32[8,1,256]{2,0,1:T(8,128)S(1)}, u32[]{:S(2)}, u32[]{:S(2)}) collective-permute-start(f32[8,1,256]{2,0,1:T(8,128)S(1)} %get-tuple-element.133), channel_id=1, source_target_pairs={{0,1},{1,2},{2,3},{4,5},{5,6},{6,7},{8,9},{9,10},{10,11},{12,13},{... | collective-permute-start | bytes 24584 | tf_op jit(solution)/shard_map/ppermute | solution.py:25
  185.1 4.1 %broadcast_in_dim.137 = f32[8,4,2,16,2,16,2]{0,6,5,4,3,2,1:T(2,128)} broadcast(f32[8,4,16,16]{0,3,2,1:T(8,128)S(1)} %bitcast.129), dimensions={0,1,3,5} | broadcast | bytes 294912 | tf_op jit(solution)/shard_map/broadcast_in_dim | solution.py:87
  194.2 4.2 %collective-permute-start.33 = (f32[8,1,1024]{2,0,1:T(8,128)S(1)}, f32[8,1,1024]{2,0,1:T(8,128)S(1)}, u32[]{:S(2)}, u32[]{:S(2)}) collective-permute-start(f32[8,1,1024]{2,0,1:T(8,128)S(1)} %get-tuple-element.113), channel_id=1, source_target_pairs={{0,1},{1,2},{2,3},{4,5},{5,6},{6,7},{8,9},{9,10},{10,11},{12,13},{... | collective-permute-start | bytes 98312 | tf_op jit(solution)/shard_map/ppermute | solution.py:25
  200.6 17.1 %while.3 = (s32[]{:T(128)}, f32[8,8,1536]{2,0,1:T(8,128)S(1)}, s32[8,3]{0,1:T(4,128)S(1)}, f32[8,8,1024]{2,0,1:T(8,128)S(1)}, s32[]{:T(128)}, /*index=5*/s32[]{:T(128)}) while((s32[]{:T(128)}, f32[8,8,1536]{2,0,1:T(8,128)S(1)}, s32[8,3]{0,1:T(4,128)S(1)}, f32[8,8,1024]{2,0,1:T(8,128)S(1)}, s32[]{:T(128)}, /*index=5*/s32[]{:T(128)}) %tuple.96), condition=%wide.while_cond.1, body=%wide.while_body.1.sunk | while | flops 2 | bytes 131197 | solution.py:120
  218.9 5.1 %collective-permute-done.34 = f32[2,8,1024]{2,0,1:T(2,128)S(1)} collective-permute-done((f32[2,8,1024]{2,0,1:T(2,128)S(1)}, f32[2,8,1024]{2,0,1:T(2,128)S(1)}, u32[]{:S(2)}, u32[]{:S(2)}) %collective-permute-start.34) | collective-permute-done | bytes 65568 | tf_op jit(solution)/shard_map/ppermute | solution.py:34
  (272 shorter events, 122.6 us)
Async XLA Ops:
  1.0 12.0 %collective-permute-start = (f32[2,4,1024]{2,0,1:T(2,128)S(1)}, f32[2,4,1024]{2,0,1:T(2,128)S(1)}, u32[]{:S(2)}, u32[]{:S(2)}) collective-permute-start(f32[2,4,1024]{2,0,1:T(2,128)S(1)} %copy.252), channel_id=1, source_target_pairs={{0,1},{1,2},{2,3},{4,5},{5,6},{6,7},{8,9},{9,10},{10,11},{12,13},{... | collective-permute-start | bytes 98312 | tf_op jit(solution)/shard_map/ppermute | solution.py:25
  5.5 8.3 %collective-permute-start.1 = (f32[2,4,1024]{2,0,1:T(2,128)S(1)}, f32[2,4,1024]{2,0,1:T(2,128)S(1)}, u32[]{:S(2)}, u32[]{:S(2)}) collective-permute-start(f32[2,4,1024]{2,0,1:T(2,128)S(1)} %copy.253), channel_id=1, source_target_pairs={{1,0},{2,1},{3,2},{5,4},{6,5},{7,6},{9,8},{10,9},{11,10},{13,12},{... | collective-permute-start | bytes 98312 | tf_op jit(solution)/shard_map/ppermute | solution.py:26
  28.6 8.4 %collective-permute-start.2 = (f32[2,20224]{1,0:T(2,128)S(1)}, f32[2,20224]{1,0:T(2,128)S(1)}, u32[]{:S(2)}, u32[]{:S(2)}) collective-permute-start(f32[2,20224]{1,0:T(2,128)S(1)} %pad_maximum_fusion.10), channel_id=1, source_target_pairs={{0,28},{4,0},{8,4},{12,8},{16,12},{20,16},{24,20},{28,24},{1,29},{... | collective-permute-start | bytes 485384 | tf_op jit(solution)/shard_map/ppermute | solution.py:34
  32.9 6.0 %collective-permute-start.3 = (f32[2,20224]{1,0:T(2,128)S(1)}, f32[2,20224]{1,0:T(2,128)S(1)}, u32[]{:S(2)}, u32[]{:S(2)}) collective-permute-start(f32[2,20224]{1,0:T(2,128)S(1)} %pad_maximum_fusion.10), channel_id=1, source_target_pairs={{0,24},{4,28},{8,0},{12,4},{16,8},{20,12},{24,16},{28,20},{1,25},{... | collective-permute-start | bytes 485384 | tf_op jit(solution)/shard_map/ppermute | solution.py:34
  59.4 6.7 %collective-permute-start.4 = (f32[8,1,1024]{2,0,1:T(8,128)S(1)}, f32[8,1,1024]{2,0,1:T(8,128)S(1)}, u32[]{:S(2)}, u32[]{:S(2)}) collective-permute-start(f32[8,1,1024]{2,0,1:T(8,128)S(1)} %get-tuple-element.124), channel_id=1, source_target_pairs={{1,0},{2,1},{3,2},{5,4},{6,5},{7,6},{9,8},{10,9},{11,10},{13,12},{... | collective-permute-start | bytes 98312 | tf_op jit(solution)/shard_map/ppermute | solution.py:26
  74.7 6.7 %collective-permute-start.6 = (f32[8,1,256]{2,0,1:T(8,128)S(1)}, f32[8,1,256]{2,0,1:T(8,128)S(1)}, u32[]{:S(2)}, u32[]{:S(2)}) collective-permute-start(f32[8,1,256]{2,0,1:T(8,128)S(1)} %get-tuple-element.138), channel_id=1, source_target_pairs={{1,0},{2,1},{3,2},{5,4},{6,5},{7,6},{9,8},{10,9},{11,10},{13,12},{... | collective-permute-start | bytes 24584 | tf_op jit(solution)/shard_map/ppermute | solution.py:26
  82.5 6.2 %collective-permute-start.8 = (f32[8,1,64]{2,0,1:T(8,128)S(1)}, f32[8,1,64]{2,0,1:T(8,128)S(1)}, u32[]{:S(2)}, u32[]{:S(2)}) collective-permute-start(f32[8,1,64]{2,0,1:T(8,128)S(1)} %get-tuple-element.150), channel_id=1, source_target_pairs={{1,0},{2,1},{3,2},{5,4},{6,5},{7,6},{9,8},{10,9},{11,10},{13,12},{... | collective-permute-start | bytes 6152 | tf_op jit(solution)/shard_map/ppermute | solution.py:26
  89.4 6.1 %collective-permute-start.10 = (f32[8,1,64]{2,0,1:T(8,128)S(1)}, f32[8,1,64]{2,0,1:T(8,128)S(1)}, u32[]{:S(2)}, u32[]{:S(2)}) collective-permute-start(f32[8,1,64]{2,0,1:T(8,128)S(1)} %get-tuple-element.148), channel_id=1, source_target_pairs={{1,0},{2,1},{3,2},{5,4},{6,5},{7,6},{9,8},{10,9},{11,10},{13,12},{... | collective-permute-start | bytes 6152 | tf_op jit(solution)/shard_map/ppermute | solution.py:26
  96.4 6.1 %collective-permute-start.12 = (f32[8,1,64]{2,0,1:T(8,128)S(1)}, f32[8,1,64]{2,0,1:T(8,128)S(1)}, u32[]{:S(2)}, u32[]{:S(2)}) collective-permute-start(f32[8,1,64]{2,0,1:T(8,128)S(1)} %get-tuple-element.146), channel_id=1, source_target_pairs={{1,0},{2,1},{3,2},{5,4},{6,5},{7,6},{9,8},{10,9},{11,10},{13,12},{... | collective-permute-start | bytes 6152 | tf_op jit(solution)/shard_map/ppermute | solution.py:26
  103.8 6.1 %collective-permute-start.14 = (f32[8,1,256]{2,0,1:T(8,128)S(1)}, f32[8,1,256]{2,0,1:T(8,128)S(1)}, u32[]{:S(2)}, u32[]{:S(2)}) collective-permute-start(f32[8,1,256]{2,0,1:T(8,128)S(1)} %get-tuple-element.136), channel_id=1, source_target_pairs={{1,0},{2,1},{3,2},{5,4},{6,5},{7,6},{9,8},{10,9},{11,10},{13,12},{... | collective-permute-start | bytes 24584 | tf_op jit(solution)/shard_map/ppermute | solution.py:26
  118.0 6.1 %collective-permute-start.16 = (f32[8,1,1024]{2,0,1:T(8,128)S(1)}, f32[8,1,1024]{2,0,1:T(8,128)S(1)}, u32[]{:S(2)}, u32[]{:S(2)}) collective-permute-start(f32[8,1,1024]{2,0,1:T(8,128)S(1)} %get-tuple-element.120), channel_id=1, source_target_pairs={{1,0},{2,1},{3,2},{5,4},{6,5},{7,6},{9,8},{10,9},{11,10},{13,12},{... | collective-permute-start | bytes 98312 | tf_op jit(solution)/shard_map/ppermute | solution.py:26
  119.9 5.2 %collective-permute-start.17 = (f32[8,1,1024]{2,0,1:T(8,128)S(1)}, f32[8,1,1024]{2,0,1:T(8,128)S(1)}, u32[]{:S(2)}, u32[]{:S(2)}) collective-permute-start(f32[8,1,1024]{2,0,1:T(8,128)S(1)} %get-tuple-element.121), channel_id=1, source_target_pairs={{0,1},{1,2},{2,3},{4,5},{5,6},{6,7},{8,9},{9,10},{10,11},{12,13},{... | collective-permute-start | bytes 98312 | tf_op jit(solution)/shard_map/ppermute | solution.py:25
  125.5 6.2 %collective-permute-start.18 = (f32[8,1,1024]{2,0,1:T(8,128)S(1)}, f32[8,1,1024]{2,0,1:T(8,128)S(1)}, u32[]{:S(2)}, u32[]{:S(2)}) collective-permute-start(f32[8,1,1024]{2,0,1:T(8,128)S(1)} %get-tuple-element.118), channel_id=1, source_target_pairs={{1,0},{2,1},{3,2},{5,4},{6,5},{7,6},{9,8},{10,9},{11,10},{13,12},{... | collective-permute-start | bytes 98312 | tf_op jit(solution)/shard_map/ppermute | solution.py:26
  127.5 5.2 %collective-permute-start.19 = (f32[8,1,1024]{2,0,1:T(8,128)S(1)}, f32[8,1,1024]{2,0,1:T(8,128)S(1)}, u32[]{:S(2)}, u32[]{:S(2)}) collective-permute-start(f32[8,1,1024]{2,0,1:T(8,128)S(1)} %get-tuple-element.119), channel_id=1, source_target_pairs={{0,1},{1,2},{2,3},{4,5},{5,6},{6,7},{8,9},{9,10},{10,11},{12,13},{... | collective-permute-start | bytes 98312 | tf_op jit(solution)/shard_map/ppermute | solution.py:25
  133.1 6.2 %collective-permute-start.20 = (f32[8,1,1024]{2,0,1:T(8,128)S(1)}, f32[8,1,1024]{2,0,1:T(8,128)S(1)}, u32[]{:S(2)}, u32[]{:S(2)}) collective-permute-start(f32[8,1,1024]{2,0,1:T(8,128)S(1)} %get-tuple-element.116), channel_id=1, source_target_pairs={{1,0},{2,1},{3,2},{5,4},{6,5},{7,6},{9,8},{10,9},{11,10},{13,12},{... | collective-permute-start | bytes 98312 | tf_op jit(solution)/shard_map/ppermute | solution.py:26
  135.1 5.2 %collective-permute-start.21 = (f32[8,1,1024]{2,0,1:T(8,128)S(1)}, f32[8,1,1024]{2,0,1:T(8,128)S(1)}, u32[]{:S(2)}, u32[]{:S(2)}) collective-permute-start(f32[8,1,1024]{2,0,1:T(8,128)S(1)} %get-tuple-element.117), channel_id=1, source_target_pairs={{0,1},{1,2},{2,3},{4,5},{5,6},{6,7},{8,9},{9,10},{10,11},{12,13},{... | collective-permute-start | bytes 98312 | tf_op jit(solution)/shard_map/ppermute | solution.py:25
  148.8 6.3 %collective-permute-start.22 = (f32[8,1,256]{2,0,1:T(8,128)S(1)}, f32[8,1,256]{2,0,1:T(8,128)S(1)}, u32[]{:S(2)}, u32[]{:S(2)}) collective-permute-start(f32[8,1,256]{2,0,1:T(8,128)S(1)} %get-tuple-element.134), channel_id=1, source_target_pairs={{1,0},{2,1},{3,2},{5,4},{6,5},{7,6},{9,8},{10,9},{11,10},{13,12},{... | collective-permute-start | bytes 24584 | tf_op jit(solution)/shard_map/ppermute | solution.py:26
  156.5 6.2 %collective-permute-start.24 = (f32[8,1,64]{2,0,1:T(8,128)S(1)}, f32[8,1,64]{2,0,1:T(8,128)S(1)}, u32[]{:S(2)}, u32[]{:S(2)}) collective-permute-start(f32[8,1,64]{2,0,1:T(8,128)S(1)} %get-tuple-element.144), channel_id=1, source_target_pairs={{1,0},{2,1},{3,2},{5,4},{6,5},{7,6},{9,8},{10,9},{11,10},{13,12},{... | collective-permute-start | bytes 6152 | tf_op jit(solution)/shard_map/ppermute | solution.py:26
  163.5 6.1 %collective-permute-start.26 = (f32[8,1,64]{2,0,1:T(8,128)S(1)}, f32[8,1,64]{2,0,1:T(8,128)S(1)}, u32[]{:S(2)}, u32[]{:S(2)}) collective-permute-start(f32[8,1,64]{2,0,1:T(8,128)S(1)} %get-tuple-element.142), channel_id=1, source_target_pairs={{1,0},{2,1},{3,2},{5,4},{6,5},{7,6},{9,8},{10,9},{11,10},{13,12},{... | collective-permute-start | bytes 6152 | tf_op jit(solution)/shard_map/ppermute | solution.py:26
  170.5 6.1 %collective-permute-start.28 = (f32[8,1,64]{2,0,1:T(8,128)S(1)}, f32[8,1,64]{2,0,1:T(8,128)S(1)}, u32[]{:S(2)}, u32[]{:S(2)}) collective-permute-start(f32[8,1,64]{2,0,1:T(8,128)S(1)} %get-tuple-element.140), channel_id=1, source_target_pairs={{1,0},{2,1},{3,2},{5,4},{6,5},{7,6},{9,8},{10,9},{11,10},{13,12},{... | collective-permute-start | bytes 6152 | tf_op jit(solution)/shard_map/ppermute | solution.py:26
  177.9 6.1 %collective-permute-start.30 = (f32[8,1,256]{2,0,1:T(8,128)S(1)}, f32[8,1,256]{2,0,1:T(8,128)S(1)}, u32[]{:S(2)}, u32[]{:S(2)}) collective-permute-start(f32[8,1,256]{2,0,1:T(8,128)S(1)} %get-tuple-element.132), channel_id=1, source_target_pairs={{1,0},{2,1},{3,2},{5,4},{6,5},{7,6},{9,8},{10,9},{11,10},{13,12},{... | collective-permute-start | bytes 24584 | tf_op jit(solution)/shard_map/ppermute | solution.py:26
  192.1 6.4 %collective-permute-start.32 = (f32[8,1,1024]{2,0,1:T(8,128)S(1)}, f32[8,1,1024]{2,0,1:T(8,128)S(1)}, u32[]{:S(2)}, u32[]{:S(2)}) collective-permute-start(f32[8,1,1024]{2,0,1:T(8,128)S(1)} %get-tuple-element.112), channel_id=1, source_target_pairs={{1,0},{2,1},{3,2},{5,4},{6,5},{7,6},{9,8},{10,9},{11,10},{13,12},{... | collective-permute-start | bytes 98312 | tf_op jit(solution)/shard_map/ppermute | solution.py:26
  218.1 5.9 %collective-permute-start.34 = (f32[2,8,1024]{2,0,1:T(2,128)S(1)}, f32[2,8,1024]{2,0,1:T(2,128)S(1)}, u32[]{:S(2)}, u32[]{:S(2)}) collective-permute-start(f32[2,8,1024]{2,0,1:T(2,128)S(1)} %convolution_add_fusion.6), channel_id=1, source_target_pairs={{0,4},{4,8},{8,12},{12,16},{16,20},{20,24},{24,28},{28,0},{1,5},{5... | collective-permute-start | bytes 196616 | tf_op jit(solution)/shard_map/ppermute | solution.py:34
  218.5 5.7 %collective-permute-start.35 = (f32[2,8,1024]{2,0,1:T(2,128)S(1)}, f32[2,8,1024]{2,0,1:T(2,128)S(1)}, u32[]{:S(2)}, u32[]{:S(2)}) collective-permute-start(f32[2,8,1024]{2,0,1:T(2,128)S(1)} %convolution_add_fusion.5), channel_id=1, source_target_pairs={{0,8},{4,12},{8,16},{12,20},{16,24},{20,28},{24,0},{28,4},{1,9},{5... | collective-permute-start | bytes 196616 | tf_op jit(solution)/shard_map/ppermute | solution.py:34
  (13 other events, 73.8 us)
where the time goes:
time: 227 us; the launch traced here: 225 us
  starting transfers between devices  103 us (45%)
  local copies, waits for them, and re-layouts  71.2 us (31%)
  waiting for transfers between devices  20.7 us (9%)
  other arithmetic  19.5 us (9%)
  matrix products  9.16 us (4%)
    ppermute x16, starting transfers between devices, extended_2(): before = lax.ppermute(last, axis, up)  67.2 us
    gather x64, local copies, waits for them, and re-layouts  33.8 us
    ppermute x16, starting transfers between devices, extended_2(): after = lax.ppermute(initial, axis, down)  30.9 us
    reduce_sum x6, other arithmetic, coarsen(): grouped.mean(axis=(2, 4, 6))  14.8 us
    ppermute x16, waiting for transfers between devices, extended_2(): before = lax.ppermute(last, axis, up)  10.5 us
    ppermute x4, waiting for transfers between devices, passed_along(): return lax.ppermute(value, axis, pairs)  10.2 us
    reshape x1, local copies, waits for them, and re-layouts, coarsen(): values.reshape(slot_count, layer_count // 2, 2, half_edge, 2, half_edge, 2)  9.81 us
    broadcast_in_dim x8, local copies, waits for them, and re-layouts, refine(): jnp.broadcast_to(values.reshape(slot_count, layer_count, 1, half_edge, 1,...  9.2 us
  transfers between devices with their start and end apart: 36, of which 18 were waited for; matrix products, arithmetic and copies ran while one was open for 4% of the time, Pallas kernels for 0%

commit v1 on v0

v1 whole, which is shorter than its diff:
```python
import functools

import jax
import jax.numpy as jnp
from jax import lax
from jax.experimental import pallas as pl
from jax.experimental.pallas import tpu as pltpu
from jax.sharding import PartitionSpec as P

PMAX = 4
SMAX = 8
CYCLES = 2
SWEEPS = 4
FOURPI = 4.0 * 3.141592653589793
OMEGA = 0.8
KEEP = 1.0 - OMEGA
LANES = 128
ROWS = 8
BEFORE = 2
AFTER = 2


def lane_roll(value, shift):
    return pltpu.roll(value, shift % LANES, value.ndim - 1)


def row_roll(value, shift):
    return pltpu.roll(value, shift % ROWS, value.ndim - 2)


def lane_bit(shape, bit):
    lane = lax.broadcasted_iota(jnp.int32, shape, len(shape) - 1)
    return ((lane >> bit) & 1) == 1


def z_up(value):
    return jnp.where(lane_bit(value.shape, 0), lane_roll(value, -31), lane_roll(value, -1))


def z_down(value):
    return jnp.where(lane_bit(value.shape, 0), lane_roll(value, 1), lane_roll(value, 31))


def swap_bits(tiles):
    tiles = list(tiles)
    for weight, bit in ((4, 6), (2, 5), (1, 0)):
        mask = lane_bit((ROWS, LANES), bit)
        step = 1 << bit
        for k in range(8):
            if not k & weight:
                a, b = tiles[k], tiles[k + weight]
                tiles[k] = jnp.where(mask, lane_roll(b, step), a)
                tiles[k + weight] = jnp.where(mask, b, lane_roll(a, -step))
    return tiles


def stack(parts):
    return jnp.concatenate([part[None] for part in parts], axis=0)


def kernel(
    n, G, own, N,
    orb_ref, eps_ref, off_ref, cnt_ref, shift_ref, out_ref,
    ibuf, ebuf, jbuf, moved, pbuf, tbuf, field, rhs, va, vb,
    kx, ky, kz, wt, dg, stage1, stage2, got1, got2,
    s_send, e_recv, i_recv, j_recv, f_send, f_recv, c_send, c_recv,
):
    per = G // own
    S = PMAX // per
    o = lax.axis_index("orb")
    g = lax.axis_index("grid")
    a_me = g // per
    h_me = lax.rem(g, per)

    def place(gr, p):
        reach = gr // per + (gr % per) * S + p + 1
        return reach // own, reach % own

    def at_orb(t):
        return lax.rem(o + (t + n), n)

    reach_t = [sorted({place(gr, p)[0] for p in range(S)} - {0}) for gr in range(G)]
    largest = max(max(ts) for ts in reach_t)

    barrier = pltpu.get_barrier_semaphore()

    def greet(orb, grid):
        pl.semaphore_signal(
            barrier, inc=1, device_id={"orb": orb, "grid": grid},
            device_id_type=pl.DeviceIdType.MESH,
        )

    for step in range(1, G):
        greet(o, lax.rem(g + step, G))
    greeted = G - 1
    for gr in range(G):
        for t in reach_t[gr]:
            greet(at_orb(-t), gr)
            greeted += 1
    expected = jnp.int32(greeted)
    for t in range(1, largest + 1):
        mine = functools.reduce(
            jnp.logical_or, [g == gr for gr in range(G) if t in reach_t[gr]]
        )

        @pl.when(mine)
        def _():
            for gr in range(G):
                greet(at_orb(t), gr)

        expected = expected + jnp.where(mine, G, 0).astype(jnp.int32)
    pl.semaphore_wait(barrier, expected)

    def send(src, dst, send_sem, recv_sem, orb, grid, is_self):
        def remote():
            return pltpu.make_async_remote_copy(
                src_ref=src, dst_ref=dst, send_sem=send_sem, recv_sem=recv_sem,
                device_id={"orb": orb, "grid": grid},
                device_id_type=pl.DeviceIdType.MESH,
            )

        if is_self is None:
            remote().start()
        else:
            @pl.when(is_self)
            def _():
                pltpu.make_async_copy(src, dst, recv_sem).start()

            @pl.when(jnp.logical_not(is_self))
            def _():
                remote().start()

        def finish():
            if is_self is None:
                remote().wait_send()
            else:
                @pl.when(jnp.logical_not(is_self))
                def _():
                    remote().wait_send()

        return finish

    pending = []
    count = 0
    mid = pl.ds(BEFORE * LANES, orb_ref.shape[2])
    for gr in range(G):
        pending.append(send(
            eps_ref.at[gr // per], ebuf.at[g], s_send.at[count], e_recv.at[g], o, gr, g == gr))
        count += 1
    for gr in range(G):
        for p in range(S):
            t, b = place(gr, p)
            pending.append(send(
                orb_ref.at[b], jbuf.at[p, g, :, mid], s_send.at[count], j_recv.at[p, g],
                at_orb(-t), gr, (g == gr) if t == 0 else None))
            count += 1
    for gr in range(G):
        pending.append(send(
            orb_ref.at[gr // per], ibuf.at[g], s_send.at[count], i_recv.at[g], o, gr, g == gr))
        count += 1

    first = o * own + a_me
    deltas, signs = [], []
    for p in range(S):
        distance = h_me * S + p + 1
        second = lax.rem(first + distance, N)
        deltas.append(shift_ref[first] - shift_ref[second])
        live = jnp.int32(0)
        for k in range(PMAX):
            hit = jnp.where(off_ref[first, k] == distance - 1, 1, 0)
            live = live + jnp.where(k < cnt_ref[first], hit, 0)
        signs.append(jnp.where(live > 0, -1.0, 0.0).astype(jnp.float32))

    wide = orb_ref.shape[2]
    tiles = wide // LANES
    for buf in (jbuf, pbuf):
        for p in range(S):
            for zh in range(G):
                buf[p, zh, :, 0 : BEFORE * LANES] = jnp.zeros((ROWS, BEFORE * LANES), jnp.float32)
                buf[p, zh, :, BEFORE * LANES + wide :] = jnp.zeros((ROWS, AFTER * LANES), jnp.float32)

    lane2 = lax.broadcasted_iota(jnp.int32, (ROWS, LANES), 1)

    def arrived(dst, sem):
        pltpu.make_async_copy(dst, dst, sem).wait()

    def load_shifted(buf, p, zh, delta):
        amount = jnp.full((ROWS, LANES), delta + SMAX, jnp.int32)
        bits = [((amount >> k) & 1) == 1 for k in range(5)]
        ext = [buf[p, zh, :, t * LANES : (t + 1) * LANES] for t in range(tiles + BEFORE + AFTER)]
        for k in (4, 3, 2):
            skip = 1 << (k - 2)
            ext = [
                jnp.where(bits[k], ext[t + skip], ext[t]) if t + skip < len(ext) else ext[t]
                for t in range(min(len(ext), tiles + skip))
            ]
        for k in (1, 0):
            step = 32 << k
            inner = lane2 < LANES - step
            turned = [lane_roll(value, -step) for value in ext]
            ext = [
                jnp.where(bits[k], jnp.where(inner, turned[t], turned[t + 1]) if t + 1 < len(ext) else turned[t], ext[t])
                for t in range(len(ext))
            ]
        return ext[:tiles]

    def to_blocked(src, dst_store):
        for zl in range(4):
            got = [
                src[k >> 1, pl.ds((k & 1) * 4 + zl, ROWS, stride=ROWS), :] for k in range(8)
            ]
            for k, value in enumerate(swap_bits(got)):
                dst_store(k >> 1, k & 1, zl, value)

    def put_tiles(dst, zh, slab):
        for yh in range(tiles):
            dst[zh, yh * ROWS : (yh + 1) * ROWS, :] = slab[:, yh * LANES : (yh + 1) * LANES]

    for zh in range(G):
        arrived(ebuf.at[zh], e_recv.at[zh])
        put_tiles(tbuf.at[S], zh, ebuf[zh])

    def store_eps(yl, x0, zl, value):
        field[yl, x0, zl] = value

    to_blocked(tbuf.at[S], store_eps)

    row2 = lax.broadcasted_iota(jnp.int32, (ROWS, LANES), 0)
    xh = (lane2 >> 1) & 15
    z8 = (lane2 >> 5) * 2 + (lane2 & 1)

    def keep(mask, value):
        return jnp.where(jnp.broadcast_to(mask, value.shape), value, 0.0)

    def face(scale, centre, beyond, mask=None):
        k = (0.5 * scale) * (centre + beyond)
        return k if mask is None else keep(mask, k)

    x_last, x_first = xh < 15, xh > 0
    y_last, y_first = row2 < 7, row2 > 0
    z_last, z_first = z8 < 7, z8 > 0

    for yl in range(4):
        e = field[yl]
        exp = stack([e[1], keep(x_last, lane_roll(e[0], -2))])
        exm = stack([keep(x_first, lane_roll(e[1], 2)), e[0]])
        eyp = field[yl + 1] if yl < 3 else keep(y_last, row_roll(field[0], -1))
        eym = field[yl - 1] if yl > 0 else keep(y_first, row_roll(field[3], 1))
        ezp = jnp.concatenate([e[:, 1:], keep(z_last, z_up(e[:, 0]))[:, None]], axis=1)
        ezm = jnp.concatenate([keep(z_first, z_down(e[:, 3]))[:, None], e[:, :3]], axis=1)
        diag = 3.0 * e + 0.5 * (((exp + exm) + (eyp + eym)) + (ezp + ezm))
        dg[yl] = diag
        wt[yl] = OMEGA / diag
        kxv = 0.5 * (e + exp)
        kx[yl, 0] = kxv[0]
        kx[yl, 1] = keep(x_last, kxv[1])
        kyv = 0.5 * (e + eyp)
        ky[yl] = kyv if yl < 3 else keep(y_last, kyv)
        kzv = 0.5 * (e + ezp)
        kz[yl, :, 0:3] = kzv[:, 0:3]
        kz[yl, :, 3] = keep(z_last, kzv[:, 3])

    def pair_sum(y0, y1):
        s = y0 + y1
        s = s[0] + s[1]
        return stack([s[0] + s[1], s[2] + s[3]])

    def to_quarter(mid_level):
        s = (mid_level[0, 0] + mid_level[0, 1]) + (mid_level[1, 0] + mid_level[1, 1])
        other = jnp.where(lane_bit(s.shape, 1), lane_roll(s, 2), lane_roll(s, -2))
        return 0.125 * (s + other)

    e1 = 0.125 * stack([pair_sum(field[0], field[1]), pair_sum(field[2], field[3])])

    def mid_y_up(v):
        return stack([v[1], row_roll(v[0], -1)])

    def mid_y_down(v):
        return stack([row_roll(v[1], 1), v[0]])

    def mid_z_up(v):
        return jnp.concatenate([v[:, 1:], z_up(v[:, 0])[:, None]], axis=1)

    def mid_z_down(v):
        return jnp.concatenate([z_down(v[:, 1])[:, None], v[:, :1]], axis=1)

    def mid_keep_y(mask, v, index):
        return stack([keep(mask, v[k]) if k == index else v[k] for k in range(2)])

    def mid_keep_z(mask, v, index):
        return jnp.concatenate(
            [(keep(mask, v[:, k]) if k == index else v[:, k])[:, None] for k in range(2)], axis=1)

    n1 = [
        keep(x_last, lane_roll(e1, -2)), keep(x_first, lane_roll(e1, 2)),
        mid_keep_y(y_last, mid_y_up(e1), 1), mid_keep_y(y_first, mid_y_down(e1), 0),
        mid_keep_z(z_last, mid_z_up(e1), 1), mid_keep_z(z_first, mid_z_down(e1), 0),
    ]
    w1 = OMEGA / (0.25 * (3.0 * e1 + 0.5 * (((n1[0] + n1[1]) + (n1[2] + n1[3])) + (n1[4] + n1[5]))))
    k1 = [face(0.25, e1, v) for v in n1]
    k1 = [
        keep(x_last, k1[0]), keep(x_first, k1[1]),
        mid_keep_y(y_last, k1[2], 1), mid_keep_y(y_first, k1[3], 0),
        mid_keep_z(z_last, k1[4], 1), mid_keep_z(z_first, k1[5], 0),
    ]
    e2 = to_quarter(e1)
    x2_last, x2_first = xh < 14, xh > 1
    masks2 = [x2_last, x2_first, y_last, y_first, z_last, z_first]

    def around2(v):
        return [lane_roll(v, -4), lane_roll(v, 4), row_roll(v, -1), row_roll(v, 1), z_up(v), z_down(v)]

    n2 = [keep(m, v) for m, v in zip(masks2, around2(e2))]
    w2 = OMEGA / (0.0625 * (3.0 * e2 + 0.5 * (((n2[0] + n2[1]) + (n2[2] + n2[3])) + (n2[4] + n2[5]))))
    k2 = [face(0.0625, e2, v, m) for m, v in zip(masks2, n2)]

    def weigh(ks, vs):
        t = [k * v for k, v in zip(ks, vs)]
        return ((t[0] + t[1]) + (t[2] + t[3])) + (t[4] + t[5])

    def off1(v):
        return weigh(k1, [lane_roll(v, -2), lane_roll(v, 2), mid_y_up(v), mid_y_down(v),
                          mid_z_up(v), mid_z_down(v)])

    def off2(v):
        return weigh(k2, around2(v))

    for zh in range(G):
        arrived(ibuf.at[zh], i_recv.at[zh])
        for p in range(S):
            arrived(jbuf.at[p, zh, :, mid], j_recv.at[p, zh])
            m = jnp.concatenate(load_shifted(jbuf, p, zh, deltas[p]), axis=1)
            moved[p, zh] = m
            put_tiles(tbuf.at[p], zh, FOURPI * (ibuf[zh] * m))
    for p in range(S):
        def store_rhs(yl, x0, zl, value):
            rhs[p, yl, x0, zl] = value

        to_blocked(tbuf.at[p], store_rhs)

    def off0(src, p, yl):
        v = src[p, yl]
        kxv, kzv = kx[yl], kz[yl]
        v0, v1 = v[0], v[1]
        xs = stack([kxv[0] * v1 + lane_roll(kxv[1] * v1, 2),
                    kxv[1] * lane_roll(v0, -2) + kxv[0] * v0])
        kv = kzv * v
        zs = kzv * jnp.concatenate([v[:, 1:], z_up(v[:, 0])[:, None]], axis=1)
        zs = zs + jnp.concatenate([z_down(kv[:, 3])[:, None], kv[:, :3]], axis=1)
        up = src[p, yl + 1] if yl < 3 else row_roll(src[p, 0], -1)
        ys = ky[yl] * up
        if yl > 0:
            ys = ys + ky[yl - 1] * src[p, yl - 1]
        else:
            ys = ys + row_roll(ky[3] * src[p, 3], 1)
        return xs + ys + zs

    def coarse(f1):
        u = w1 * f1
        f2 = to_quarter(KEEP * f1 + off1(u))
        t = w2 * f2
        for _ in range(SWEEPS - 1):
            t = KEEP * t + w2 * (f2 + off2(t))
        u = u + t
        return KEEP * u + w1 * (f1 + off1(u))

    def relax0(src, dst, p):
        for yl in range(4):
            dst[p, yl] = KEEP * src[p, yl] + wt[yl] * (rhs[p, yl] + off0(src, p, yl))

    for cycle in range(CYCLES):
        if cycle == 0:
            for p in range(S):
                for yl in range(4):
                    vb[p, yl] = wt[yl] * rhs[p, yl]
        else:
            for p in range(S):
                relax0(va, vb, p)
        coarse_rhs = []
        for p in range(S):
            rows = []
            for yh in range(2):
                res = []
                for yl in (2 * yh, 2 * yh + 1):
                    if cycle == 0:
                        res.append(KEEP * rhs[p, yl] + off0(vb, p, yl))
                    else:
                        res.append(rhs[p, yl] - dg[yl] * vb[p, yl] + off0(vb, p, yl))
                rows.append(pair_sum(res[0], res[1]))
            coarse_rhs.append(0.125 * stack(rows))
        corrections = [coarse(f1) for f1 in coarse_rhs]
        for p in range(S):
            for yl in range(4):
                c = corrections[p][yl // 2]
                grown = stack([c[0], c[0], c[1], c[1]])
                vb[p, yl] = vb[p, yl] + grown[None]
            relax0(vb, va, p)

    for p in range(S):
        for zl in range(4):
            got = [va[p, k >> 1, k & 1, zl] for k in range(8)]
            for k, value in enumerate(swap_bits(got)):
                tbuf[p, k >> 1, pl.ds((k & 1) * 4 + zl, ROWS, stride=ROWS), :] = value

    reaches = [a_me + h_me * S + p + 1 for p in range(S)]
    count = 0
    for zh in range(G):
        total = None
        for p in range(S):
            pot = jnp.concatenate(
                [tbuf[p, zh, yh * ROWS : (yh + 1) * ROWS, :] for yh in range(tiles)], axis=1)
            pot = signs[p] * pot
            term = pot * moved[p, zh]
            total = term if total is None else total + term
            pbuf[p, zh, :, mid] = pot * ibuf[zh]
            stage2[p, zh] = jnp.concatenate(load_shifted(pbuf, p, zh, -deltas[p]), axis=1)
            t = reaches[p] // own
            pending.append(send(
                stage2.at[p, zh], got2.at[g, p], c_send.at[p, zh], c_recv.at[g, p],
                lax.rem(o + t, n), zh, jnp.logical_and(t == 0, g == zh)))
        stage1[zh] = total
        pending.append(send(
            stage1.at[zh], got1.at[g], f_send.at[zh], f_recv.at[g], o, zh, g == zh))

    sums = [None] * own
    for gr in range(G):
        arrived(got1.at[gr], f_recv.at[gr])
        value = got1[gr]
        b = gr // per
        sums[b] = value if sums[b] is None else sums[b] + value
    for gr in range(G):
        for p in range(S):
            arrived(got2.at[gr, p], c_recv.at[gr, p])
            b = place(gr, p)[1]
            sums[b] = sums[b] + got2[gr, p]
    for b in range(own):
        out_ref[b] = sums[b]
    for finish in pending:
        finish()


def solution(mesh):
    n, G = mesh.shape["orb"], mesh.shape["grid"]

    def shards(orbitals, dielectric, pair_offsets, pair_counts, box_shift):
        own, rows, wide = orbitals.shape
        N = pair_counts.shape[0]
        S = own * PMAX // G
        padded = wide + (BEFORE + AFTER) * LANES
        f32 = jnp.float32
        blocked = (4, 2, 4, ROWS, LANES)
        smem = pl.BlockSpec(memory_space=pltpu.SMEM)
        hbm = pl.BlockSpec(memory_space=pl.ANY)
        dma = pltpu.SemaphoreType.DMA
        return pl.pallas_call(
            functools.partial(kernel, n, G, own, N),
            out_shape=jax.ShapeDtypeStruct(orbitals.shape, f32),
            in_specs=[hbm, hbm, smem, smem, smem],
            out_specs=pl.BlockSpec(memory_space=pltpu.VMEM),
            scratch_shapes=[
                pltpu.VMEM((G, rows, wide), f32),
                pltpu.VMEM((G, rows, wide), f32),
                pltpu.VMEM((S, G, rows, padded), f32),
                pltpu.VMEM((S, G, rows, wide), f32),
                pltpu.VMEM((S, G, rows, padded), f32),
                pltpu.VMEM((S + 1, G, rows * wide // LANES, LANES), f32),
                pltpu.VMEM(blocked, f32),
                pltpu.VMEM((S,) + blocked, f32),
                pltpu.VMEM((S,) + blocked, f32),
                pltpu.VMEM((S,) + blocked, f32),
                pltpu.VMEM(blocked, f32),
                pltpu.VMEM(blocked, f32),
                pltpu.VMEM(blocked, f32),
                pltpu.VMEM(blocked, f32),
                pltpu.VMEM(blocked, f32),
                pltpu.VMEM((G, rows, wide), f32),
                pltpu.VMEM((S, G, rows, wide), f32),
                pltpu.VMEM((G, rows, wide), f32),
                pltpu.VMEM((G, S, rows, wide), f32),
                dma((G * (S + 2),)),
                dma((G,)),
                dma((G,)),
                dma((S, G)),
                dma((G,)),
                dma((G,)),
                dma((S, G)),
                dma((G, S)),
            ],
            compiler_params=pltpu.CompilerParams(
                collective_id=0, has_side_effects=True, vmem_limit_bytes=24 * 1024 * 1024
            ),
        )(orbitals, dielectric, pair_offsets, pair_counts, box_shift)

    placed = (P("orb", "grid", None), P("orb", "grid", None), P(), P(), P())
    return jax.shard_map(
        shards, mesh=mesh, in_specs=placed, out_specs=P("orb", "grid", None), check_vma=False
    )
```

time: 227 us -> 28.9 us (0.13)
  starting transfers between devices: 103 us -> 0 us
  local copies, waits for them, and re-layouts: 71.2 us -> 3.1 us
  Pallas kernels: 0 us -> 25.6 us
  waiting for transfers between devices: 20.7 us -> 0 us
  other arithmetic: 19.5 us -> 0 us
  matrix products: 9.16 us -> 0 us
    ppermute x36 -> x0, starting transfers between devices: 103 us -> none  [the longest x16 67.2 us: extended_2(): before = lax.ppermute(last, axis, up)]
    gather x64 -> x0, local copies, waits for them, and re-layouts: 33.8 us -> none
    pallas_call x0 -> x1, Pallas kernels: none -> 25.6 us  [shards(): pl.pallas_call(functools.partial(kernel, n, G, own, N), out_shape=jax.Sha...]
    ppermute x36 -> x0, waiting for transfers between devices: 20.7 us -> none  [the longest x16 10.5 us: extended_2(): before = lax.ppermute(last, axis, up)]
    reshape x8 -> x0, local copies, waits for them, and re-layouts: 15.9 us -> none  [the longest x1 9.81 us: coarsen(): values.reshape(slot_count, layer_count // 2, 2, half_edge, 2, half_edge, 2)]
    reduce_sum x8 -> x0, other arithmetic: 15.9 us -> none  [the longest x6 14.8 us: coarsen(): grouped.mean(axis=(2, 4, 6))]
    broadcast_in_dim x10 -> x0, local copies, waits for them, and re-layouts: 9.29 us -> none  [the longest x8 9.2 us: refine(): jnp.broadcast_to(values.reshape(slot_count, layer_count, 1, half_edge, 1,...]
    dot_general x21 -> x0, matrix products: 9.16 us -> none  [the longest x12 5.42 us: shards(): jnp.einsum('sa,azf->szf', first_hot, portion, precision=HIGHEST)]
  transfers between devices with their start and end apart: 36 -> 0, of which waited for: 18 -> 0; matrix products, arithmetic and copies ran while one was open for 4% -> 0% of each run, Pallas kernels for 0% -> 0%
where the time goes in v1:
time: 28.9 us; the launch traced here: 28.7 us
  Pallas kernels  25.6 us (89%)
  local copies, waits for them, and re-layouts  3.1 us (11%)
    pallas_call x1, Pallas kernels, shards(): pl.pallas_call(functools.partial(kernel, n, G, own, N), out_shape=jax.Sha...  25.6 us
    unnamed x10, local copies, waits for them, and re-layouts  3.1 us

profile of v1, /device:TPU:1, one launch (start us, length us, event | category | flops | bytes accessed | tf_op | source)
XLA Modules:
  0.0 28.7 jit_solution(549641377301712930)
XLA Ops:
  0.0 0.0 copy-start.3
  0.0 0.0 copy-start.2
  0.0 0.8 %copy.6.off_ref = s32[16,4]{1,0:T(8,128)S(1)} copy(s32[16,4]{0,1:T(4,128)} %param.7) | data formatting | bytes 512 | tf_op args[2]
  0.8 0.0 copy-done.3
  0.8 0.0 copy-done.2
  0.8 0.0 copy-start
  0.8 0.8 %copy-done = f32[2,8,1024]{2,1,0:T(8,128)S(1)} copy-done((f32[2,8,1024]{2,1,0:T(8,128)S(1)}, f32[2,8,1024]{2,1,0:T(8,128)}, u32[]{:S(2)}) %copy-start) | copy-done | bytes 65560
  1.6 0.0 copy-start.1
  1.6 0.8 %copy-done.1 = f32[2,8,1024]{2,1,0:T(8,128)S(1)} copy-done((f32[2,8,1024]{2,1,0:T(8,128)S(1)}, f32[2,8,1024]{2,1,0:T(8,128)}, u32[]{:S(2)}) %copy-start.1) | copy-done | bytes 65560
  2.5 25.6 %shard_map.55 = f32[2,8,1024]{2,1,0:T(8,128)S(1)} custom-call(f32[2,8,1024]{2,1,0:T(8,128)S(1)} %copy-done, f32[2,8,1024]{2,1,0:T(8,128)S(1)} %copy-done.1, s32[16,4]{1,0:T(8,128)S(1)} %copy.6.off_ref, s32[16]{0:T(128)S(1)} %copy-done.2, s32[16]{0:T(128)S(1)} %copy-done.3), custom_call_target="tpu_custom_call" | custom-call | tf_op jit(solution)/shard_map/pallas_call | solution.py:455
  28.1 0.6 %copy.8 = f32[2,8,1024]{2,1,0:T(8,128)} copy(f32[2,8,1024]{2,1,0:T(8,128)S(1)} %shard_map.55) | data formatting | bytes 131072
Async XLA Ops:
  0.0 0.8 %copy-start.3 = (s32[16]{0:T(128)S(1)}, s32[16]{0:T(128)}, u32[]{:S(2)}) copy-start(s32[16]{0:T(128)} %shift_ref.1) | copy-start | bytes 196
  0.0 0.8 %copy-start.2 = (s32[16]{0:T(128)S(1)}, s32[16]{0:T(128)}, u32[]{:S(2)}) copy-start(s32[16]{0:T(128)} %cnt_ref.1) | copy-start | bytes 196
  0.8 0.8 %copy-start = (f32[2,8,1024]{2,1,0:T(8,128)S(1)}, f32[2,8,1024]{2,1,0:T(8,128)}, u32[]{:S(2)}) copy-start(f32[2,8,1024]{2,1,0:T(8,128)} %orb_ref.1) | copy-start | bytes 196612
  1.6 0.8 %copy-start.1 = (f32[2,8,1024]{2,1,0:T(8,128)S(1)}, f32[2,8,1024]{2,1,0:T(8,128)}, u32[]{:S(2)}) copy-start(f32[2,8,1024]{2,1,0:T(8,128)} %eps_ref.1) | copy-start | bytes 196612

commit v2 on v1

--- a/solution.py
+++ b/solution.py
@@ -148,16 +148,16 @@
             eps_ref.at[gr // per], ebuf.at[g], s_send.at[count], e_recv.at[g], o, gr, g == gr))
         count += 1
     for gr in range(G):
-        for p in range(S):
+        pending.append(send(
+            orb_ref.at[gr // per], ibuf.at[g], s_send.at[count], i_recv.at[g], o, gr, g == gr))
+        count += 1
+    for p in range(S):
+        for gr in range(G):
             t, b = place(gr, p)
             pending.append(send(
                 orb_ref.at[b], jbuf.at[p, g, :, mid], s_send.at[count], j_recv.at[p, g],
                 at_orb(-t), gr, (g == gr) if t == 0 else None))
             count += 1
-    for gr in range(G):
-        pending.append(send(
-            orb_ref.at[gr // per], ibuf.at[g], s_send.at[count], i_recv.at[g], o, gr, g == gr))
-        count += 1
 
     first = o * own + a_me
     deltas, signs = [], []
@@ -167,7 +167,7 @@
         deltas.append(shift_ref[first] - shift_ref[second])
         live = jnp.int32(0)
         for k in range(PMAX):
-            hit = jnp.where(off_ref[first, k] == distance - 1, 1, 0)
+            hit = jnp.where(off_ref[k, first] == distance - 1, 1, 0)
             live = live + jnp.where(k < cnt_ref[first], hit, 0)
         signs.append(jnp.where(live > 0, -1.0, 0.0).astype(jnp.float32))
 
@@ -325,19 +325,6 @@
     def off2(v):
         return weigh(k2, around2(v))
 
-    for zh in range(G):
-        arrived(ibuf.at[zh], i_recv.at[zh])
-        for p in range(S):
-            arrived(jbuf.at[p, zh, :, mid], j_recv.at[p, zh])
-            m = jnp.concatenate(load_shifted(jbuf, p, zh, deltas[p]), axis=1)
-            moved[p, zh] = m
-            put_tiles(tbuf.at[p], zh, FOURPI * (ibuf[zh] * m))
-    for p in range(S):
-        def store_rhs(yl, x0, zl, value):
-            rhs[p, yl, x0, zl] = value
-
-        to_blocked(tbuf.at[p], store_rhs)
-
     def off0(src, p, yl):
         v = src[p, yl]
         kxv, kzv = kx[yl], kz[yl]
@@ -368,16 +355,13 @@
         for yl in range(4):
             dst[p, yl] = KEEP * src[p, yl] + wt[yl] * (rhs[p, yl] + off0(src, p, yl))
 
-    for cycle in range(CYCLES):
-        if cycle == 0:
-            for p in range(S):
+    def solve(p):
+        for cycle in range(CYCLES):
+            if cycle == 0:
                 for yl in range(4):
                     vb[p, yl] = wt[yl] * rhs[p, yl]
-        else:
-            for p in range(S):
+            else:
                 relax0(va, vb, p)
-        coarse_rhs = []
-        for p in range(S):
             rows = []
             for yh in range(2):
                 res = []
@@ -387,40 +371,46 @@
                     else:
                         res.append(rhs[p, yl] - dg[yl] * vb[p, yl] + off0(vb, p, yl))
                 rows.append(pair_sum(res[0], res[1]))
-            coarse_rhs.append(0.125 * stack(rows))
-        corrections = [coarse(f1) for f1 in coarse_rhs]
-        for p in range(S):
+            correction = coarse(0.125 * stack(rows))
             for yl in range(4):
-                c = corrections[p][yl // 2]
+                c = correction[yl // 2]
                 grown = stack([c[0], c[0], c[1], c[1]])
                 vb[p, yl] = vb[p, yl] + grown[None]
             relax0(vb, va, p)
 
     for p in range(S):
+        for zh in range(G):
+            if p == 0:
+                arrived(ibuf.at[zh], i_recv.at[zh])
+            arrived(jbuf.at[p, zh, :, mid], j_recv.at[p, zh])
+            m = jnp.concatenate(load_shifted(jbuf, p, zh, deltas[p]), axis=1)
+            moved[p, zh] = m
+            put_tiles(tbuf.at[p], zh, FOURPI * (ibuf[zh] * m))
+
+        def store_rhs(yl, x0, zl, value):
+            rhs[p, yl, x0, zl] = value
+
+        to_blocked(tbuf.at[p], store_rhs)
+        solve(p)
         for zl in range(4):
             got = [va[p, k >> 1, k & 1, zl] for k in range(8)]
             for k, value in enumerate(swap_bits(got)):
                 tbuf[p, k >> 1, pl.ds((k & 1) * 4 + zl, ROWS, stride=ROWS), :] = value
-
-    reaches = [a_me + h_me * S + p + 1 for p in range(S)]
-    count = 0
-    for zh in range(G):
-        total = None
-        for p in range(S):
+        t = (a_me + h_me * S + p + 1) // own
+        for zh in range(G):
             pot = jnp.concatenate(
                 [tbuf[p, zh, yh * ROWS : (yh + 1) * ROWS, :] for yh in range(tiles)], axis=1)
             pot = signs[p] * pot
-            term = pot * moved[p, zh]
-            total = term if total is None else total + term
             pbuf[p, zh, :, mid] = pot * ibuf[zh]
             stage2[p, zh] = jnp.concatenate(load_shifted(pbuf, p, zh, -deltas[p]), axis=1)
-            t = reaches[p] // own
             pending.append(send(
                 stage2.at[p, zh], got2.at[g, p], c_send.at[p, zh], c_recv.at[g, p],
                 lax.rem(o + t, n), zh, jnp.logical_and(t == 0, g == zh)))
-        stage1[zh] = total
-        pending.append(send(
-            stage1.at[zh], got1.at[g], f_send.at[zh], f_recv.at[g], o, zh, g == zh))
+            term = pot * moved[p, zh]
+            stage1[zh] = term if p == 0 else stage1[zh] + term
+            if p == S - 1:
+                pending.append(send(
+                    stage1.at[zh], got1.at[g], f_send.at[zh], f_recv.at[g], o, zh, g == zh))
 
     sums = [None] * own
     for gr in range(G):
@@ -450,7 +440,7 @@
         f32 = jnp.float32
         blocked = (4, 2, 4, ROWS, LANES)
         smem = pl.BlockSpec(memory_space=pltpu.SMEM)
-        hbm = pl.BlockSpec(memory_space=pl.ANY)
+        hbm = pl.BlockSpec(memory_space=pltpu.HBM)
         dma = pltpu.SemaphoreType.DMA
         return pl.pallas_call(
             functools.partial(kernel, n, G, own, N),
@@ -487,9 +477,9 @@
                 dma((G, S)),
             ],
             compiler_params=pltpu.CompilerParams(
-                collective_id=0, has_side_effects=True, vmem_limit_bytes=24 * 1024 * 1024
+                collective_id=0, has_side_effects=True, vmem_limit_bytes=63 * 1024 * 1024
             ),
-        )(orbitals, dielectric, pair_offsets, pair_counts, box_shift)
+        )(orbitals, dielectric, pair_offsets.T, pair_counts, box_shift)
 
     placed = (P("orb", "grid", None), P("orb", "grid", None), P(), P(), P())
     return jax.shard_map(

time: 28.9 us -> 27.6 us (0.955)
  local copies, waits for them, and re-layouts: 3.1 us -> 1.47 us
  Pallas kernels: 25.6 us -> 25.9 us
    unnamed x10 -> x1, local copies, waits for them, and re-layouts: 3.1 us -> 1.47 us
where the time goes in v2:
time: 27.6 us; the launch traced here: 27.3 us
  Pallas kernels  25.9 us (94%)
  local copies, waits for them, and re-layouts  1.47 us (5%)
    pallas_call x1, Pallas kernels, shards(): pl.pallas_call(functools.partial(kernel, n, G, own, N), out_shape=jax.Sha...  25.9 us
    unnamed x1, local copies, waits for them, and re-layouts  1.47 us

profile of v2, /device:TPU:1, one launch (start us, length us, event | category | flops | bytes accessed | tf_op | source)
XLA Modules:
  0.0 27.3 jit_solution(14329140395141409508)
XLA Ops:
  0.0 25.9 %shard_map.55 = f32[2,8,1024]{2,1,0:T(8,128)} custom-call(f32[2,8,1024]{2,1,0:T(8,128)} %orb_ref.1, f32[2,8,1024]{2,1,0:T(8,128)} %eps_ref.1, s32[4,16]{1,0:T(4,128)} %bitcast.1, s32[16]{0:T(128)} %cnt_ref.1, s32[16]{0:T(128)} %shift_ref.1), custom_call_target="tpu_custom_call" | custom-call | tf_op jit(solution)/shard_map/pallas_call | solution.py:445
  25.9 1.5 %copy.7 = f32[2,8,1024]{2,1,0:T(8,128)} copy(f32[2,8,1024]{2,1,0:T(8,128)} %shard_map.55) | data formatting | bytes 131072

commit v3 on v2

--- a/solution.py
+++ b/solution.py
@@ -63,7 +63,7 @@
     orb_ref, eps_ref, off_ref, cnt_ref, shift_ref, out_ref,
     ibuf, ebuf, jbuf, moved, pbuf, tbuf, field, rhs, va, vb,
     kx, ky, kz, wt, dg, stage1, stage2, got1, got2,
-    s_send, e_recv, i_recv, j_recv, f_send, f_recv, c_send, c_recv,
+    b_send, b_recv, j_send, j_recv, f_send, f_recv, c_send, c_recv,
 ):
     per = G // own
     S = PMAX // per
@@ -111,53 +111,44 @@
         expected = expected + jnp.where(mine, G, 0).astype(jnp.int32)
     pl.semaphore_wait(barrier, expected)
 
-    def send(src, dst, send_sem, recv_sem, orb, grid, is_self):
-        def remote():
-            return pltpu.make_async_remote_copy(
-                src_ref=src, dst_ref=dst, send_sem=send_sem, recv_sem=recv_sem,
-                device_id={"orb": orb, "grid": grid},
-                device_id_type=pl.DeviceIdType.MESH,
-            )
-
-        if is_self is None:
-            remote().start()
-        else:
-            @pl.when(is_self)
-            def _():
-                pltpu.make_async_copy(src, dst, recv_sem).start()
-
-            @pl.when(jnp.logical_not(is_self))
-            def _():
-                remote().start()
-
-        def finish():
-            if is_self is None:
-                remote().wait_send()
-            else:
-                @pl.when(jnp.logical_not(is_self))
-                def _():
-                    remote().wait_send()
-
-        return finish
-
-    pending = []
-    count = 0
+    def remote(src, dst, send_sem, recv_sem, orb, grid):
+        pltpu.make_async_remote_copy(
+            src_ref=src, dst_ref=dst, send_sem=send_sem, recv_sem=recv_sem,
+            device_id={"orb": orb, "grid": grid}, device_id_type=pl.DeviceIdType.MESH,
+        ).start()
+
+    def local(src, dst, recv_sem):
+        pltpu.make_async_copy(src, dst, recv_sem).start()
+
+    def arrived(whole, sem):
+        pltpu.make_async_copy(whole, whole, sem).wait()
+
+    def own_slot(p):
+        found = [gr for gr in range(G) if place(gr, p)[0] == 0]
+        return found[0] if found else None
+
     mid = pl.ds(BEFORE * LANES, orb_ref.shape[2])
-    for gr in range(G):
-        pending.append(send(
-            eps_ref.at[gr // per], ebuf.at[g], s_send.at[count], e_recv.at[g], o, gr, g == gr))
-        count += 1
-    for gr in range(G):
-        pending.append(send(
-            orb_ref.at[gr // per], ibuf.at[g], s_send.at[count], i_recv.at[g], o, gr, g == gr))
-        count += 1
+    others = [lax.rem(g + step, G) for step in range(1, G)]
+    for field_ref, buf, which in ((eps_ref, ebuf, 0), (orb_ref, ibuf, 1)):
+        for gr in others:
+            remote(field_ref.at[gr // per], buf.at[g], b_send.at[which], b_recv.at[which], o, gr)
+        local(field_ref.at[a_me], buf.at[g], b_recv.at[which])
     for p in range(S):
         for gr in range(G):
             t, b = place(gr, p)
-            pending.append(send(
-                orb_ref.at[b], jbuf.at[p, g, :, mid], s_send.at[count], j_recv.at[p, g],
-                at_orb(-t), gr, (g == gr) if t == 0 else None))
-            count += 1
+            src, dst = orb_ref.at[b], jbuf.at[p, g, :, mid]
+
+            def to_other(src=src, dst=dst, t=t, gr=gr, p=p):
+                remote(src, dst, j_send.at[p], j_recv.at[p], at_orb(-t), gr)
+
+            if gr == own_slot(p):
+                pl.when(g != gr)(to_other)
+
+                @pl.when(g == gr)
+                def _(src=src, dst=dst, p=p):
+                    local(src, dst, j_recv.at[p])
+            else:
+                to_other()
 
     first = o * own + a_me
     deltas, signs = [], []
@@ -180,9 +171,6 @@
                 buf[p, zh, :, BEFORE * LANES + wide :] = jnp.zeros((ROWS, AFTER * LANES), jnp.float32)
 
     lane2 = lax.broadcasted_iota(jnp.int32, (ROWS, LANES), 1)
-
-    def arrived(dst, sem):
-        pltpu.make_async_copy(dst, dst, sem).wait()
 
     def load_shifted(buf, p, zh, delta):
         amount = jnp.full((ROWS, LANES), delta + SMAX, jnp.int32)
@@ -216,8 +204,8 @@
         for yh in range(tiles):
             dst[zh, yh * ROWS : (yh + 1) * ROWS, :] = slab[:, yh * LANES : (yh + 1) * LANES]
 
+    arrived(ebuf, b_recv.at[0])
     for zh in range(G):
-        arrived(ebuf.at[zh], e_recv.at[zh])
         put_tiles(tbuf.at[S], zh, ebuf[zh])
 
     def store_eps(yl, x0, zl, value):
@@ -379,10 +367,10 @@
             relax0(vb, va, p)
 
     for p in range(S):
+        if p == 0:
+            arrived(ibuf, b_recv.at[1])
+        arrived(jbuf.at[p, :, :, mid], j_recv.at[p])
         for zh in range(G):
-            if p == 0:
-                arrived(ibuf.at[zh], i_recv.at[zh])
-            arrived(jbuf.at[p, zh, :, mid], j_recv.at[p, zh])
             m = jnp.concatenate(load_shifted(jbuf, p, zh, deltas[p]), axis=1)
             moved[p, zh] = m
             put_tiles(tbuf.at[p], zh, FOURPI * (ibuf[zh] * m))
@@ -403,30 +391,53 @@
             pot = signs[p] * pot
             pbuf[p, zh, :, mid] = pot * ibuf[zh]
             stage2[p, zh] = jnp.concatenate(load_shifted(pbuf, p, zh, -deltas[p]), axis=1)
-            pending.append(send(
-                stage2.at[p, zh], got2.at[g, p], c_send.at[p, zh], c_recv.at[g, p],
-                lax.rem(o + t, n), zh, jnp.logical_and(t == 0, g == zh)))
+            def to_other(p=p, zh=zh, t=t):
+                remote(stage2.at[p, zh], got2.at[g, p], c_send.at[p], c_recv, lax.rem(o + t, n), zh)
+
+            if zh == own_slot(p):
+                pl.when(g != zh)(to_other)
+
+                @pl.when(g == zh)
+                def _(p=p, zh=zh):
+                    local(stage2.at[p, zh], got2.at[g, p], c_recv)
+            else:
+                to_other()
             term = pot * moved[p, zh]
             stage1[zh] = term if p == 0 else stage1[zh] + term
-            if p == S - 1:
-                pending.append(send(
-                    stage1.at[zh], got1.at[g], f_send.at[zh], f_recv.at[g], o, zh, g == zh))
+    for zh in others:
+        remote(stage1.at[zh], got1.at[g], f_send, f_recv, o, zh)
+    local(stage1.at[g], got1.at[g], f_recv)
+
+    arrived(ebuf.at[pl.ds(0, G - 1)], b_send.at[0])
+    arrived(ibuf.at[pl.ds(0, G - 1)], b_send.at[1])
+    for whole, sem in ((ebuf, j_send), (stage1, c_send)):
+        for p in range(S):
+            gr = own_slot(p)
+            if gr is None:
+                arrived(whole, sem.at[p])
+            else:
+                @pl.when(g != gr)
+                def _(whole=whole, sem=sem, p=p):
+                    arrived(whole, sem.at[p])
+
+                @pl.when(g == gr)
+                def _(whole=whole, sem=sem, p=p):
+                    arrived(whole.at[pl.ds(0, G - 1)], sem.at[p])
+    arrived(stage1.at[pl.ds(0, G - 1)], f_send)
 
     sums = [None] * own
-    for gr in range(G):
-        arrived(got1.at[gr], f_recv.at[gr])
-        value = got1[gr]
-        b = gr // per
-        sums[b] = value if sums[b] is None else sums[b] + value
+    arrived(got2, c_recv)
     for gr in range(G):
         for p in range(S):
-            arrived(got2.at[gr, p], c_recv.at[gr, p])
             b = place(gr, p)[1]
-            sums[b] = sums[b] + got2[gr, p]
+            value = got2[gr, p]
+            sums[b] = value if sums[b] is None else sums[b] + value
+    arrived(got1, f_recv)
+    for gr in range(G):
+        b = gr // per
+        sums[b] = sums[b] + got1[gr]
     for b in range(own):
         out_ref[b] = sums[b]
-    for finish in pending:
-        finish()
 
 
 def solution(mesh):
@@ -467,14 +478,14 @@
                 pltpu.VMEM((S, G, rows, wide), f32),
                 pltpu.VMEM((G, rows, wide), f32),
                 pltpu.VMEM((G, S, rows, wide), f32),
-                dma((G * (S + 2),)),
-                dma((G,)),
-                dma((G,)),
-                dma((S, G)),
-                dma((G,)),
-                dma((G,)),
-                dma((S, G)),
-                dma((G, S)),
+                dma((2,)),
+                dma((2,)),
+                dma((S,)),
+                dma((S,)),
+                dma(()),
+                dma(()),
+                dma((S,)),
+                dma(()),
             ],
             compiler_params=pltpu.CompilerParams(
                 collective_id=0, has_side_effects=True, vmem_limit_bytes=63 * 1024 * 1024

time: 27.6 us -> 26.9 us (0.975)
  Pallas kernels: 25.9 us -> 25 us
    pallas_call x1, Pallas kernels: 25.9 us -> 25 us  [shards(): pl.pallas_call(functools.partial(kernel, n, G, own, N), out_shape=jax.Sha...]
where the time goes in v3:
time: 26.9 us; the launch traced here: 26.5 us
  Pallas kernels  25 us (93%)
  local copies, waits for them, and re-layouts  1.47 us (5%)
    pallas_call x1, Pallas kernels, shards(): pl.pallas_call(functools.partial(kernel, n, G, own, N), out_shape=jax.Sha...  25 us
    unnamed x1, local copies, waits for them, and re-layouts  1.47 us

profile of v3, /device:TPU:1, one launch (start us, length us, event | category | flops | bytes accessed | tf_op | source)
XLA Modules:
  0.0 26.5 jit_solution(8431061711549382059)
XLA Ops:
  0.0 25.0 %shard_map.55 = f32[2,8,1024]{2,1,0:T(8,128)} custom-call(f32[2,8,1024]{2,1,0:T(8,128)} %orb_ref.1, f32[2,8,1024]{2,1,0:T(8,128)} %eps_ref.1, s32[4,16]{1,0:T(4,128)} %bitcast.1, s32[16]{0:T(128)} %cnt_ref.1, s32[16]{0:T(128)} %shift_ref.1), custom_call_target="tpu_custom_call" | custom-call | tf_op jit(solution)/shard_map/pallas_call | solution.py:456
  25.0 1.5 %copy.7 = f32[2,8,1024]{2,1,0:T(8,128)} copy(f32[2,8,1024]{2,1,0:T(8,128)} %shard_map.55) | data formatting | bytes 131072
